TPU v7x, 32 devices: a whole 2x2x4 slice. The times are simulated.
32 devices in a mesh: grp: 4 (over y, core), blk: 8 (over z, x).
Axes of the slice: x: 2, y: 2, z: 4, core: 2. Of those that a mesh axis runs over, the one named last changes fastest.
Arguments:
- hidden_in: bfloat16 [8, 512, 1024], P('blk', 'grp'), may hold values from -6 to 6
- attn_gain: float32 [1024], replicated, may hold values from 0.1 to 1.9
- qkv_weight: bfloat16 [1024, 3, 16, 64], P(None, None, 'grp'), may hold values from -0.09375 to 0.09375
- rel_bias: float32 [32, 16], P(None, 'grp'), may hold values from -4 to 4
- prefix_cache: bfloat16 [8, 256, 2, 16, 64], P('blk', None, None, 'grp'), may hold values from -34 to 34
- prefix_owner: int32 [8], replicated, may hold values from 0 to 7, each once
- req_prefix: int32 [8, 2], replicated, may hold values from 0 to 7
- req_pages: int32 [8, 2], replicated, may hold values from 1 to 12, 16 in all within a row
- page_table: int32 [8, 16], replicated, may hold values from 0 to 15, each once within a row
- proj_weight: bfloat16 [1024, 1024], replicated, may hold values from -0.1875 to 0.1875
- mlp_gain: float32 [1024], replicated, may hold values from 0.1 to 1.9
- in_weight: bfloat16 [1024, 4096], P(None, 'grp'), may hold values from -0.1875 to 0.1875
- out_weight: bfloat16 [4096, 1024], P('grp'), may hold values from -0.09375 to 0.09375
Outputs:
- hidden_out: bfloat16 [8, 512, 1024], P('blk', 'grp')
- suffix_cache: bfloat16 [8, 512, 2, 16, 64], P('blk', None, None, 'grp')
Inputs may be any that keep to these rules, and one draw needn't show every extreme that they name: Prefix p's keys and values are row prefix_owner[p] of prefix_cache; every owner column holds one prefix. `req_pages`: each row sums to 16 and no entry exceeds 12. `page_table`: each row is a permutation of the logical pages of a column.
All inputs are finite; a program needn't handle non-finite values.
Results may differ from a plain program's by a relative error of at most 0.012.
Values may be sent and summed in bfloat16 or wider, within the bound.
A program may use at most 128 MiB of HBM per device.

v0:
```python
import jax
import jax.numpy as jnp
from jax import lax
from jax.sharding import PartitionSpec as P

PAGE = 32
EPSILON = 1e-06
THRESHOLDS = (12, 16, 23, 32, 46, 64, 91)


def rms_scale(values, gain):
    mean_sq = jnp.mean(values * values, axis=-1, keepdims=True)
    return values * lax.rsqrt(mean_sq + EPSILON) * gain


def bucket_of(relative):
    magnitude = jnp.abs(relative)
    steps_up = jnp.zeros(relative.shape, jnp.int32)
    for limit in THRESHOLDS:
        steps_up = steps_up + (magnitude >= limit).astype(jnp.int32)
    bucket = jnp.where(magnitude < 8, magnitude, jnp.minimum(8 + steps_up, 15))
    return bucket + 16 * (relative > 0).astype(jnp.int32)


def token_meta(pages_row, lengths_row, page_size, prefix_len):
    inclusive = jnp.cumsum(lengths_row, dtype=jnp.int32)
    exclusive = inclusive - lengths_row
    request = jnp.sum(
        (pages_row[:, None] >= inclusive[None, :]).astype(jnp.int32), axis=1, dtype=jnp.int32
    )
    slot_ids = jnp.arange(lengths_row.shape[0], dtype=jnp.int32)
    start = jnp.sum(
        jnp.where(request[:, None] == slot_ids[None, :], exclusive[None, :], 0),
        axis=1,
        dtype=jnp.int32,
    )
    offsets = (pages_row - start) * page_size + prefix_len
    within = jnp.arange(page_size, dtype=jnp.int32)
    positions = (offsets[:, None] + within[None, :]).reshape(-1)
    requests = jnp.broadcast_to(request[:, None], (request.shape[0], page_size)).reshape(-1)
    return (requests, positions)


def attend_block(queries, key_rows, value_rows, query_req, query_pos, key_req, key_pos, rel_bias):
    scores = jnp.einsum("qhd,khd->hqk", queries, key_rows, preferred_element_type=jnp.float32)
    bucket = bucket_of(key_pos[None, :] - query_pos[:, None])
    bias_add = jnp.zeros(scores.shape, jnp.float32)
    for bucket_id in range(rel_bias.shape[0]):
        bias_add = jnp.where(
            (bucket == bucket_id)[None], rel_bias[bucket_id][:, None, None], bias_add
        )
    allowed = (key_req[None, :] == query_req[:, None])[None]
    scores = jnp.where(allowed, scores + bias_add, -1e30)
    row_max = jnp.max(scores, axis=-1, keepdims=True)
    weights = jnp.exp(scores - row_max)
    weights = (weights / jnp.sum(weights, axis=-1, keepdims=True)).astype(jnp.bfloat16)
    return jnp.einsum(
        "hqk,khd->qhd", weights, value_rows, preferred_element_type=jnp.float32
    ).astype(jnp.bfloat16)


def shards(
    hidden_in,
    attn_gain,
    qkv_weight,
    rel_bias,
    prefix_cache,
    prefix_owner,
    req_prefix,
    req_pages,
    page_table,
    proj_weight,
    mlp_gain,
    in_weight,
    out_weight,
):
    width = hidden_in.shape[2]
    heads_dev = qkv_weight.shape[2]
    head_dim = qkv_weight.shape[3]
    inner = heads_dev * head_dim
    residual = hidden_in[0].astype(jnp.float32)
    normed = rms_scale(residual, attn_gain).astype(jnp.bfloat16)
    qkv_flat = qkv_weight.reshape(width, 3 * inner)
    projected = jnp.dot(
        lax.all_gather(normed, "grp", axis=0, tiled=True),
        qkv_flat,
        preferred_element_type=jnp.float32,
    ).astype(jnp.bfloat16)
    column_tok = projected.shape[0]
    projected = projected.reshape(column_tok, 3, heads_dev, head_dim)
    suffix_cache = projected[:, 1:3][None]
    column = lax.axis_index("blk")
    requests_col = req_prefix.shape[1]
    prefix_ids = jnp.arange(prefix_owner.shape[0], dtype=jnp.int32)
    owner_cols = jnp.sum(
        jnp.where(
            req_prefix[:, :, None] == prefix_ids[None, None, :], prefix_owner[None, None, :], 0
        ),
        axis=2,
        dtype=jnp.int32,
    )
    my_cols = lax.dynamic_index_in_dim(owner_cols, column, 0, keepdims=False)
    prefix_len = prefix_cache.shape[1]
    slot_width = 2 * inner
    local_slot = prefix_cache.reshape(prefix_len, slot_width)
    gathered = lax.all_gather(local_slot[None], "blk", axis=0, tiled=True)
    prefix_rows = jnp.take(gathered, my_cols, axis=0)
    prefix_rows = prefix_rows.reshape(requests_col * prefix_len, 2, heads_dev, head_dim)
    key_rows = jnp.concatenate([prefix_rows[:, 0], projected[:, 1]], axis=0)
    value_rows = jnp.concatenate([prefix_rows[:, 1], projected[:, 2]], axis=0)
    pages_row = lax.dynamic_index_in_dim(page_table, column, 0, keepdims=False)
    lengths_row = lax.dynamic_index_in_dim(req_pages, column, 0, keepdims=False)
    query_req, query_pos = token_meta(pages_row, lengths_row, PAGE, prefix_len)
    slot_ids = jnp.arange(requests_col, dtype=jnp.int32)
    key_req = jnp.concatenate([jnp.repeat(slot_ids, prefix_len), query_req])
    key_pos = jnp.concatenate(
        [jnp.tile(jnp.arange(prefix_len, dtype=jnp.int32), requests_col), query_pos]
    )
    block_rows = min(512, column_tok)
    block_count = column_tok // block_rows

    def one_block(operands):
        block_q, block_req, block_pos = operands
        return attend_block(
            block_q, key_rows, value_rows, block_req, block_pos, key_req, key_pos, rel_bias
        )

    attended = lax.map(
        one_block,
        (
            projected[:, 0].reshape(block_count, block_rows, heads_dev, head_dim),
            query_req.reshape(block_count, block_rows),
            query_pos.reshape(block_count, block_rows),
        ),
    )
    attended = attended.reshape(1, column_tok, inner)
    token_heads = lax.all_to_all(attended, "grp", split_axis=1, concat_axis=2, tiled=True)[0]
    mixed = residual + jnp.dot(token_heads, proj_weight, preferred_element_type=jnp.float32)
    normed_mlp = rms_scale(mixed, mlp_gain).astype(jnp.bfloat16)
    activated = jax.nn.relu(
        jnp.dot(
            lax.all_gather(normed_mlp, "grp", axis=0, tiled=True),
            in_weight,
            preferred_element_type=jnp.float32,
        )
    ).astype(jnp.bfloat16)
    summed = lax.psum_scatter(
        jnp.dot(activated, out_weight, preferred_element_type=jnp.float32).astype(jnp.bfloat16),
        "grp",
        scatter_dimension=0,
        tiled=True,
    ).astype(jnp.float32)
    hidden_out = (mixed + summed).astype(jnp.bfloat16)[None]
    return (hidden_out, suffix_cache)


def solution(mesh):
    return jax.shard_map(
        shards,
        mesh=mesh,
        in_specs=(
            P("blk", "grp", None),
            P(),
            P(None, None, "grp", None),
            P(None, "grp"),
            P("blk", None, None, "grp", None),
            P(),
            P(),
            P(),
            P(),
            P(),
            P(),
            P(None, "grp"),
            P("grp", None),
        ),
        out_specs=(P("blk", "grp", None), P("blk", None, None, "grp", None)),
        check_vma=False,
    )
```

profile of v0, /device:TPU:0, one launch (start us, length us, event | category | flops | bytes accessed | tf_op | source)
XLA Modules:
  0.0 208.7 jit_solution(3867273368891614869)
XLA Ops:
  7.2 1.2 fusion.11
  8.5 1.8 fusion.13
  10.3 1.8 copy.46
  14.0 1.9 slice_reduce_fusion.31
  15.9 1.6 slice_reduce_fusion.30
  19.7 1.2 broadcast_compare_fusion.32
  20.9 17.4 %broadcast_compare_fusion.25 = (pred[512,1024]{1,0:T(8,128)(4,1)}, pred[512,1024]{1,0:T(8,128)(4,1)}, pred[512,1024]{1,0:T(8,128)(4,1)}, pred[512,1024]{1,0:T(8,...) fusion(s32[512]{0:T(512)S(1)} %add.896, ...), kind=kLoop, calls=%fused_computation.47 | loop fusion | flops 31981568 | bytes 16783360 | tf_op jit(solution)/shard_map/while/body/eval_jaxpr/eq | solution.py:50
  38.3 3.7 %convolution_convert_fusion.1 = bf16[512,768]{1,0:T(8,128)(2,1)} fusion(bf16[512,1024]{1,0:T(8,128)(2,1)} %all-gather.6.cloned.1.call-done, bf16[1024,768]{0,1:T(8,128)(2,1)} %bitcast.76), kind=kOutput, calls=%fused_computation.19 | convolution fusion | flops 805699584 | bytes 3407872 | tf_op jit(solution)/shard_map/dot_general | solution.py:84
  42.1 1.4 copy.48
  44.3 37.0 %all-gather.4.cloned.1.call-done = bf16[8,256,512]{2,1,0:T(8,128)(2,1)} async-done(((bf16[1,256,512]{2,1,0:T(8,128)(2,1)}), bf16[8,256,512]{2,1,0:T(8,128)(2,1)}) %all-gather.4.cloned.1.call-update) | async-done | bytes 2097168 | tf_op jit(solution)/shard_map/all_gather | solution.py:106
  81.3 2.2 %gather_fusion = bf16[2,256,512]{2,1,0:T(8,128)(2,1)S(1)} fusion(bf16[8,256,512]{2,1,0:T(8,128)(2,1)} %all-gather.4.cloned.1.call-done, s32[1024]{0:T(1024)S(1)} %pad_clamp_fusion), kind=kCustom, calls=%fused_computation | custom fusion | bytes 1048584 | tf_op jit(solution)/shard_map/jit(_take)/gather | solution.py:107
  84.6 1.4 gather.7
  86.1 29.9 %add_select_fusion = f32[4,512,1024]{2,1,0:T(8,128)} fusion(f32[4]{0:T(128)S(1)} %get-tuple-element.62, f32[4]{0:T(128)S(1)} %get-tuple-element.63, f32[4]{0:T(128)S(1)} %get-tuple-element.23, f32[4]{0:T(128)S(1)} %get-tuple-element.24, f32[4]{0:T(128)S(1)} %get-tuple-element.25, f32[4]{0:T(128)S(1)} %get-tuple-element.26, f32[4]{0:T(128)S(1)} %get-tuple-element.27, ...), kind=kOutput, calls=%fused_computation.4 | convolution fusion | flops 340787200 | bytes 26492928 | tf_op jit(solution)/shard_map/while/body/eval_jaxpr/qhd,khd->hqk/dot_general | solution.py:45
  116.0 7.5 %fusion.30 = f32[4,512]{1,0:T(4,128)S(1)} fusion(f32[4,512,1024]{2,1,0:T(8,128)} %add_select_fusion), kind=kOutput, calls=%fused_computation.138 | output fusion | flops 4195327 | bytes 8396800 | tf_op jit(solution)/shard_map/while/body/eval_jaxpr/sub | solution.py:55
  123.5 10.5 %fusion.10 = bf16[4,64,512]{2,1,0:T(8,128)(2,1)} fusion(f32[4,512]{1,0:T(4,128)S(1)} %fusion.30, bf16[512,4,64]{0,2,1:T(8,128)(2,1)S(1)} %copy-done.1, bf16[512,4,64]{0,2,1:T(8,128)(2,1)S(1)} %get-tuple-element.66, f32[4,512,1024]{2,1,0:T(8,128)} %add_select_fusion), kind=kOutput, calls=%fused_computation.21 | convolution fusion | flops 275909632 | bytes 9183232 | tf_op jit(solution)/shard_map/while/body/eval_jaxpr/hqk,khd->qhd/dot_general | solution.py:57
  134.0 1.3 copy.50
  135.8 2.9 %reduce.67 = bf16[512,256]{1,0:T(8,128)(2,1)} reduce(bf16[512,1,256]{2,1,0:T(2,128)(2,1)S(1)} %bitcast.69, bf16[]{:T(256)} %broadcast.2960), dimensions={1}, to_apply=%bitcast.52.reduce_sub_computation | reduce | bytes 524290
  139.8 9.1 %all_to_all.15 = bf16[4,2,16384]{2,1,0:T(2,128)(2,1)} all-to-all(bf16[4,2,16384]{2,1,0:T(2,128)(2,1)S(1)} %reshape.1101), channel_id=1, replica_groups=mesh['grp'=4,'blk'=8] {'grp'}, dimensions={0} | all-to-all | bytes 524288 | tf_op jit(solution)/shard_map/all_to_all | solution.py:137
  150.8 1.8 copy.51
  152.6 2.2 %multiply_reduce_fusion = (f32[128]{0:T(128)S(1)}, f32[128,1024]{1,0:T(8,128)S(1)}) fusion(bf16[128,1024]{0,1:T(8,128)(2,1)} %bitcast.71, bf16[1024,1024]{1,0:T(8,128)(2,1)} %param.22, bf16[1,128,1024]{2,1,0:T(8,128)(2,1)} %param.13), kind=kOutput, calls=%fused_computation.69 | convolution fusion | flops 268959616 | bytes 3146240 | tf_op jit(solution)/shard_map/dot_general | solution.py:138
  155.7 14.4 %all-gather.8.cloned.1.call-done = bf16[512,1024]{1,0:T(8,128)(2,1)} async-done(((bf16[128,1024]{1,0:T(8,128)(2,1)}), bf16[512,1024]{1,0:T(8,128)(2,1)}) %all-gather.8.cloned.1.call-update) | async-done | bytes 1048592 | tf_op jit(solution)/shard_map/all_gather | solution.py:142
  170.1 5.2 %convolution_convert_fusion = bf16[512,1024]{1,0:T(8,128)(2,1)} fusion(bf16[1024,1024]{1,0:T(8,128)(2,1)S(1)} %copy-done, bf16[512,1024]{1,0:T(8,128)(2,1)} %all-gather.8.cloned.1.call-done, bf16[1024,1024]{1,0:T(8,128)(2,1)} %param.24), kind=kOutput, calls=%fused_computation.18 | convolution fusion | flops 2149056512 | bytes 6291456 | tf_op jit(solution)/shard_map/dot_general | solution.py:148
  176.2 24.2 %reduce-scatter.2.cloned.1.call-done = bf16[128,1024]{1,0:T(8,128)(2,1)} async-done(((bf16[512,1024]{1,0:T(8,128)(2,1)}), bf16[128,1024]{1,0:T(8,128)(2,1)}) %reduce-scatter.2.cloned.1.call-update) | async-done | bytes 262160 | tf_op jit(solution)/shard_map/reduce_scatter | solution.py:147
  200.4 1.7 fusion.20
  (51 shorter events, 11.5 us)
Async XLA Ops:
  7.2 163.0 %copy-start = (bf16[1024,1024]{1,0:T(8,128)(2,1)S(1)}, bf16[1024,1024]{1,0:T(8,128)(2,1)}, u32[]{:S(2)}) copy-start(bf16[1024,1024]{1,0:T(8,128)(2,1)} %param.25) | copy-start | bytes 6291460
  7.2 31.1 %all-gather.6.cloned.1.call-start = ((), (), s32[]{:S(2)}) async-start(), calls=%async_computation.3 | async-start | bytes 1310720 | tf_op jit(solution)/shard_map/all_gather | solution.py:85
  10.3 71.0 %all-gather.4.cloned.1.call-start = ((), (), s32[]{:S(2)}) async-start(), calls=%async_computation.2 | async-start | bytes 2359296 | tf_op jit(solution)/shard_map/all_gather | solution.py:106
  12.2 158.0 %all-gather.8.cloned.1.call-start = ((), (), s32[]{:S(2)}) async-start(), calls=%async_computation.4 | async-start | bytes 1310720 | tf_op jit(solution)/shard_map/all_gather | solution.py:142
  116.0 7.5 %copy-start.1 = (bf16[512,4,64]{0,2,1:T(8,128)(2,1)S(1)}, bf16[512,4,64]{0,2,1:T(8,128)(2,1)}, u32[]{:S(2)}) copy-start(bf16[512,4,64]{0,2,1:T(8,128)(2,1)} %get-tuple-element.64) | copy-start | bytes 786436
  150.1 4.8 %copy-start.2 = (f32[1024]{0:T(1024)S(1)}, f32[1024]{0:T(1024)}, u32[]{:S(2)}) copy-start(f32[1024]{0:T(1024)} %param.23) | copy-start | bytes 12292
  155.7 44.8 %reduce-scatter.2.cloned.1.call-start = ((), (), s32[]{:S(2)}) async-start(), calls=%async_computation.5 | async-start | bytes 1310720 | tf_op jit(solution)/shard_map/reduce_scatter | solution.py:147
Sparse Core Ops, SparseCore 0:
  10.4 19.4 all-gather.5
  32.0 49.2 all-gather.3
  155.8 14.2 all-gather.7
  175.5 24.8 reduce-scatter.1
where the time goes:
time: 209 us
  waiting for transfers between devices  75.7 us (36%)
  matrix products  51.6 us (25%)
  other arithmetic  36.6 us (18%)
  local copies, waits for them, and re-layouts  21.6 us (10%)
  between operations  13.9 us (7%)
  blocking collectives  9.1 us (4%)
    all_gather x1, waiting for transfers between devices, shards(): gathered = lax.all_gather(local_slot[None], 'blk', axis=0, tiled=True)  37 us
    dot_general x1, matrix products, attend_block(): jnp.einsum('qhd,khd->hqk', queries, key_rows, preferred_element_type=jnp....  29.9 us
    reduce_scatter x1, waiting for transfers between devices, shards(): lax.psum_scatter(jnp.dot(activated, out_weight, preferred_element_type=jn...  24.2 us
    eq x1, other arithmetic, attend_block(): bucket == bucket_id  17.4 us
    all_gather x1, waiting for transfers between devices, shards(): lax.all_gather(normed_mlp, 'grp', axis=0, tiled=True)  14.4 us
    dot_general x1, matrix products, attend_block(): jnp.einsum('hqk,khd->qhd', weights, value_rows, preferred_element_type=jn...  10.5 us
    all_to_all x1, blocking collectives, shards(): lax.all_to_all(attended, 'grp', split_axis=1, concat_axis=2, tiled=True)[0]  9.1 us
    sub x1, other arithmetic, attend_block(): weights = jnp.exp(scores - row_max)  7.51 us
  transfers between devices with their start and end apart: 4, of which 3 were waited for; matrix products, arithmetic and copies ran while one was open for 17% of the time, Pallas kernels for 0%

commit v1 on v0

--- a/solution.py
+++ b/solution.py
@@ -6,6 +6,17 @@
 PAGE = 32
 EPSILON = 1e-06
 THRESHOLDS = (12, 16, 23, 32, 46, 64, 91)
+
+
+def gather_by_hops(value, axis, dim):
+    size = lax.axis_size(axis)
+    route = [(i, (i + 1) % size) for i in range(size)]
+    terms = [value]
+    for hop in range(1, size):
+        terms = [lax.ppermute(terms[0], axis, route), *terms]
+    full = jnp.concatenate(terms, axis=dim)
+    offset = (lax.axis_index(axis) + 1) * terms[-1].shape[dim]
+    return jnp.roll(full, offset, axis=dim)
 
 
 def rms_scale(values, gain):
@@ -103,7 +114,7 @@
     prefix_len = prefix_cache.shape[1]
     slot_width = 2 * inner
     local_slot = prefix_cache.reshape(prefix_len, slot_width)
-    gathered = lax.all_gather(local_slot[None], "blk", axis=0, tiled=True)
+    gathered = gather_by_hops(local_slot[None], "blk", 0)
     prefix_rows = jnp.take(gathered, my_cols, axis=0)
     prefix_rows = prefix_rows.reshape(requests_col * prefix_len, 2, heads_dev, head_dim)
     key_rows = jnp.concatenate([prefix_rows[:, 0], projected[:, 1]], axis=0)

time: 209 us -> 224 us (1.072)
  local copies, waits for them, and re-layouts: 21.6 us -> 28.9 us
  waiting for transfers between devices: 75.7 us -> 79.8 us
  starting transfers between devices: 0.16 us -> 3.18 us
    ppermute x0 -> x7, waiting for transfers between devices: none -> 41.6 us  [gather_by_hops(): terms = [lax.ppermute(terms[0], axis, route), *terms]]
    all_gather x1 -> x0, waiting for transfers between devices: 37 us -> none  [shards(): gathered = lax.all_gather(local_slot[None], 'blk', axis=0, tiled=True)]
    unnamed x15 -> x44, local copies, waits for them, and re-layouts: 3.57 us -> 12.4 us
    ppermute x0 -> x7, starting transfers between devices: none -> 3.06 us  [gather_by_hops(): terms = [lax.ppermute(terms[0], axis, route), *terms]]
    slice x2, local copies, waits for them, and re-layouts: 3.47 us -> 0.91 us  [attend_block(): rel_bias[bucket_id][:, None, None]]
  transfers between devices with their start and end apart: 4 -> 10, of which waited for: 3 -> 8; matrix products, arithmetic and copies ran while one was open for 17% -> 15% of each run, Pallas kernels for 0% -> 0%
where the time goes in v1:
time: 224 us; the launch traced here: 223 us
  waiting for transfers between devices  79.8 us (36%)
  matrix products  51.5 us (23%)
  other arithmetic  36.4 us (16%)
  local copies, waits for them, and re-layouts  28.9 us (13%)
  between operations  14.1 us (6%)
  blocking collectives  9.1 us (4%)
  starting transfers between devices  3.18 us (1%)
    ppermute x7, waiting for transfers between devices, gather_by_hops(): terms = [lax.ppermute(terms[0], axis, route), *terms]  41.6 us
    dot_general x1, matrix products, attend_block(): jnp.einsum('qhd,khd->hqk', queries, key_rows, preferred_element_type=jnp....  29.9 us
    reduce_scatter x1, waiting for transfers between devices, shards(): lax.psum_scatter(jnp.dot(activated, out_weight, preferred_element_type=jn...  24.2 us
    eq x1, other arithmetic, attend_block(): bucket == bucket_id  17.3 us
    all_gather x1, waiting for transfers between devices, shards(): lax.all_gather(normed_mlp, 'grp', axis=0, tiled=True)  13.9 us
    unnamed x44, local copies, waits for them, and re-layouts  12.4 us
    dot_general x1, matrix products, attend_block(): jnp.einsum('hqk,khd->qhd', weights, value_rows, preferred_element_type=jn...  10.5 us
    all_to_all x1, blocking collectives, shards(): lax.all_to_all(attended, 'grp', split_axis=1, concat_axis=2, tiled=True)[0]  9.1 us
  transfers between devices with their start and end apart: 10, of which 8 were waited for; matrix products, arithmetic and copies ran while one was open for 15% of the time, Pallas kernels for 0%

profile of v1, /device:TPU:0, one launch (start us, length us, event | category | flops | bytes accessed | tf_op | source)
XLA Modules:
  0.0 223.0 jit_solution(12961201421874763104)
XLA Ops:
  8.5 3.0 %collective-permute-start = (bf16[1,256,512]{2,1,0:T(8,128)(2,1)S(1)}, bf16[1,256,512]{2,1,0:T(8,128)(2,1)S(1)}, u32[]{:S(2)}, u32[]{:S(2)}) collective-permute-start(bf16[1,256,512]{2,1,0:T(8,128)(2,1)S(1)} %copy.52), channel_id=1, source_target_pairs={{0,1},{1,2},{2,3},{3,4},{4,5},{5,6},{6,7},{7,0},{8,9},{9,10},{10,1... | collective-permute-start | bytes 786440 | tf_op jit(solution)/shard_map/ppermute | solution.py:16
  12.5 1.8 fusion.13
  18.0 2.8 %collective-permute-done = bf16[1,256,512]{2,1,0:T(8,128)(2,1)S(1)} collective-permute-done((bf16[1,256,512]{2,1,0:T(8,128)(2,1)S(1)}, bf16[1,256,512]{2,1,0:T(8,128)(2,1)S(1)}, u32[]{:S(2)}, u32[]{:S(2)}) %collective-permute-start) | collective-permute-done | bytes 262176 | tf_op jit(solution)/shard_map/ppermute | solution.py:16
  21.0 10.0 %collective-permute-done.1 = bf16[1,256,512]{2,1,0:T(8,128)(2,1)S(1)} collective-permute-done((bf16[1,256,512]{2,1,0:T(8,128)(2,1)S(1)}, bf16[1,256,512]{2,1,0:T(8,128)(2,1)S(1)}, u32[]{:S(2)}, u32[]{:S(2)}) %collective-permute-start.1) | collective-permute-done | bytes 262176 | tf_op jit(solution)/shard_map/ppermute | solution.py:16
  31.0 17.3 %broadcast_compare_fusion.25 = (pred[512,1024]{1,0:T(8,128)(4,1)}, pred[512,1024]{1,0:T(8,128)(4,1)}, pred[512,1024]{1,0:T(8,128)(4,1)}, pred[512,1024]{1,0:T(8,...) fusion(s32[512]{0:T(512)S(1)} %add.912, ...), kind=kLoop, calls=%fused_computation.47 | loop fusion | flops 31981568 | bytes 16783360 | tf_op jit(solution)/shard_map/while/body/eval_jaxpr/eq | solution.py:61
  49.3 8.3 %collective-permute-done.3 = bf16[1,256,512]{2,1,0:T(8,128)(2,1)S(1)} collective-permute-done((bf16[1,256,512]{2,1,0:T(8,128)(2,1)S(1)}, bf16[1,256,512]{2,1,0:T(8,128)(2,1)S(1)}, u32[]{:S(2)}, u32[]{:S(2)}) %collective-permute-start.3) | collective-permute-done | bytes 262176 | tf_op jit(solution)/shard_map/ppermute | solution.py:16
  57.8 9.0 %collective-permute-done.4 = bf16[1,256,512]{2,1,0:T(8,128)(2,1)} collective-permute-done((bf16[1,256,512]{2,1,0:T(8,128)(2,1)S(1)}, bf16[1,256,512]{2,1,0:T(8,128)(2,1)}, u32[]{:S(2)}, u32[]{:S(2)}) %collective-permute-start.4) | collective-permute-done | bytes 262176 | tf_op jit(solution)/shard_map/ppermute | solution.py:16
  68.1 8.1 %collective-permute-done.5 = bf16[1,256,512]{2,1,0:T(8,128)(2,1)} collective-permute-done((bf16[1,256,512]{2,1,0:T(8,128)(2,1)}, bf16[1,256,512]{2,1,0:T(8,128)(2,1)}, u32[]{:S(2)}, u32[]{:S(2)}) %collective-permute-start.5) | collective-permute-done | bytes 262176 | tf_op jit(solution)/shard_map/ppermute | solution.py:16
  76.2 3.7 %convolution_convert_fusion.1 = bf16[512,768]{1,0:T(8,128)(2,1)} fusion(bf16[512,1024]{1,0:T(8,128)(2,1)} %all-gather.3.cloned.1.call-done, bf16[1024,768]{0,1:T(8,128)(2,1)} %bitcast.76), kind=kOutput, calls=%fused_computation.19 | convolution fusion | flops 805699584 | bytes 3407872 | tf_op jit(solution)/shard_map/dot_general | solution.py:95
  79.9 1.4 copy.56
  82.2 3.4 %collective-permute-done.6 = bf16[1,256,512]{2,1,0:T(8,128)(2,1)} collective-permute-done((bf16[1,256,512]{2,1,0:T(8,128)(2,1)}, bf16[1,256,512]{2,1,0:T(8,128)(2,1)}, u32[]{:S(2)}, u32[]{:S(2)}) %collective-permute-start.6) | collective-permute-done | bytes 262176 | tf_op jit(solution)/shard_map/ppermute | solution.py:16
  94.6 1.6 constant_dynamic-slice_fusion.2
  96.1 2.2 gather_fusion
  100.9 29.9 %add_select_fusion = f32[4,512,1024]{2,1,0:T(8,128)} fusion(f32[4]{0:T(128)S(1)} %get-tuple-element.62, f32[4]{0:T(128)S(1)} %get-tuple-element.63, f32[4]{0:T(128)S(1)} %get-tuple-element.23, f32[4]{0:T(128)S(1)} %get-tuple-element.24, f32[4]{0:T(128)S(1)} %get-tuple-element.25, f32[4]{0:T(128)S(1)} %get-tuple-element.26, f32[4]{0:T(128)S(1)} %get-tuple-element.27, ...), kind=kOutput, calls=%fused_computation.4 | convolution fusion | flops 340787200 | bytes 26492928 | tf_op jit(solution)/shard_map/while/body/eval_jaxpr/qhd,khd->hqk/dot_general | solution.py:56
  130.8 7.5 %fusion.30 = f32[4,512]{1,0:T(4,128)S(1)} fusion(f32[4,512,1024]{2,1,0:T(8,128)} %add_select_fusion), kind=kOutput, calls=%fused_computation.155 | output fusion | flops 4195327 | bytes 8396800 | tf_op jit(solution)/shard_map/while/body/eval_jaxpr/sub | solution.py:66
  138.4 10.5 %fusion.10 = bf16[4,64,512]{2,1,0:T(8,128)(2,1)} fusion(f32[4,512]{1,0:T(4,128)S(1)} %fusion.30, bf16[512,4,64]{0,2,1:T(8,128)(2,1)S(1)} %copy-done.8, bf16[512,4,64]{0,2,1:T(8,128)(2,1)S(1)} %get-tuple-element.66, f32[4,512,1024]{2,1,0:T(8,128)} %add_select_fusion), kind=kOutput, calls=%fused_computation.21 | convolution fusion | flops 275909632 | bytes 9183232 | tf_op jit(solution)/shard_map/while/body/eval_jaxpr/hqk,khd->qhd/dot_general | solution.py:68
  150.7 2.9 %reduce.67 = bf16[512,256]{1,0:T(8,128)(2,1)} reduce(bf16[512,1,256]{2,1,0:T(2,128)(2,1)S(1)} %bitcast.69, bf16[]{:T(256)} %broadcast.2961), dimensions={1}, to_apply=%bitcast.52.reduce_sub_computation | reduce | bytes 524290
  154.6 9.1 %all_to_all.15 = bf16[4,2,16384]{2,1,0:T(2,128)(2,1)} all-to-all(bf16[4,2,16384]{2,1,0:T(2,128)(2,1)S(1)} %reshape.1101), channel_id=1, replica_groups=mesh['grp'=4,'blk'=8] {'grp'}, dimensions={0} | all-to-all | bytes 524288 | tf_op jit(solution)/shard_map/all_to_all | solution.py:148
  165.6 1.8 copy.59
  167.4 2.2 multiply_reduce_fusion
  170.5 13.9 %all-gather.5.cloned.1.call-done = bf16[512,1024]{1,0:T(8,128)(2,1)} async-done(((bf16[128,1024]{1,0:T(8,128)(2,1)}), bf16[512,1024]{1,0:T(8,128)(2,1)}) %all-gather.5.cloned.1.call-update) | async-done | bytes 1048592 | tf_op jit(solution)/shard_map/all_gather | solution.py:153
  184.4 5.2 %convolution_convert_fusion = bf16[512,1024]{1,0:T(8,128)(2,1)} fusion(bf16[1024,1024]{1,0:T(8,128)(2,1)S(1)} %copy-done, bf16[512,1024]{1,0:T(8,128)(2,1)} %all-gather.5.cloned.1.call-done, bf16[1024,1024]{1,0:T(8,128)(2,1)} %param.24), kind=kOutput, calls=%fused_computation.18 | convolution fusion | flops 2149056512 | bytes 6291456 | tf_op jit(solution)/shard_map/dot_general | solution.py:159
  190.5 24.2 %reduce-scatter.2.cloned.1.call-done = bf16[128,1024]{1,0:T(8,128)(2,1)} async-done(((bf16[512,1024]{1,0:T(8,128)(2,1)}), bf16[128,1024]{1,0:T(8,128)(2,1)}) %reduce-scatter.2.cloned.1.call-update) | async-done | bytes 262160 | tf_op jit(solution)/shard_map/reduce_scatter | solution.py:158
  214.8 1.7 fusion.20
  (93 shorter events, 27.4 us)
Async XLA Ops:
  7.2 177.3 %copy-start = (bf16[1024,1024]{1,0:T(8,128)(2,1)S(1)}, bf16[1024,1024]{1,0:T(8,128)(2,1)}, u32[]{:S(2)}) copy-start(bf16[1024,1024]{1,0:T(8,128)(2,1)} %param.25) | copy-start | bytes 6291460
  7.2 69.0 %all-gather.3.cloned.1.call-start = ((), (), s32[]{:S(2)}) async-start(), calls=%async_computation.2 | async-start | bytes 1310720 | tf_op jit(solution)/shard_map/all_gather | solution.py:96
  8.5 12.3 %collective-permute-start = (bf16[1,256,512]{2,1,0:T(8,128)(2,1)S(1)}, bf16[1,256,512]{2,1,0:T(8,128)(2,1)S(1)}, u32[]{:S(2)}, u32[]{:S(2)}) collective-permute-start(bf16[1,256,512]{2,1,0:T(8,128)(2,1)S(1)} %copy.52), channel_id=1, source_target_pairs={{0,1},{1,2},{2,3},{3,4},{4,5},{5,6},{6,7},{7,0},{8,9},{9,10},{10,1... | collective-permute-start | bytes 786440 | tf_op jit(solution)/shard_map/ppermute | solution.py:16
  14.4 170.1 %all-gather.5.cloned.1.call-start = ((), (), s32[]{:S(2)}) async-start(), calls=%async_computation.3 | async-start | bytes 1310720 | tf_op jit(solution)/shard_map/all_gather | solution.py:153
  20.8 10.2 %collective-permute-start.1 = (bf16[1,256,512]{2,1,0:T(8,128)(2,1)S(1)}, bf16[1,256,512]{2,1,0:T(8,128)(2,1)S(1)}, u32[]{:S(2)}, u32[]{:S(2)}) collective-permute-start(bf16[1,256,512]{2,1,0:T(8,128)(2,1)S(1)} %collective-permute-done), channel_id=1, source_target_pairs={{0,1},{1,2},{2,3},{3,4},{4,5},{5,6},{6,7},{7,0},{8,9},{9,10},{10,1... | collective-permute-start | bytes 786440 | tf_op jit(solution)/shard_map/ppermute | solution.py:16
  21.0 27.4 %copy-start.1 = (f32[32,4]{0,1:T(4,128)S(1)}, f32[32,4]{0,1:T(4,128)}, u32[]{:S(2)}) copy-start(f32[32,4]{0,1:T(4,128)} %param.16) | copy-start | bytes 1540
  31.0 17.3 %copy-start.2 = (bf16[1,256,512]{2,1,0:T(8,128)(2,1)}, bf16[1,256,512]{2,1,0:T(8,128)(2,1)S(1)}, u32[]{:S(2)}) copy-start(bf16[1,256,512]{2,1,0:T(8,128)(2,1)S(1)} %collective-permute-done.1) | copy-start | bytes 786436
  31.0 17.3 %collective-permute-start.2 = (bf16[1,256,512]{2,1,0:T(8,128)(2,1)S(1)}, bf16[1,256,512]{2,1,0:T(8,128)(2,1)S(1)}, u32[]{:S(2)}, u32[]{:S(2)}) collective-permute-start(bf16[1,256,512]{2,1,0:T(8,128)(2,1)S(1)} %collective-permute-done.1), channel_id=1, source_target_pairs={{0,1},{1,2},{2,3},{3,4},{4,5},{5,6},{6,7},{7,0},{8,9},{9,10},{10,1... | collective-permute-start | bytes 786440 | tf_op jit(solution)/shard_map/ppermute | solution.py:16
  48.3 27.9 %copy-start.4 = (bf16[1,256,512]{2,1,0:T(8,128)(2,1)}, bf16[1,256,512]{2,1,0:T(8,128)(2,1)S(1)}, u32[]{:S(2)}) copy-start(bf16[1,256,512]{2,1,0:T(8,128)(2,1)S(1)} %collective-permute-done.2) | copy-start | bytes 786436
  48.3 9.3 %collective-permute-start.3 = (bf16[1,256,512]{2,1,0:T(8,128)(2,1)S(1)}, bf16[1,256,512]{2,1,0:T(8,128)(2,1)S(1)}, u32[]{:S(2)}, u32[]{:S(2)}) collective-permute-start(bf16[1,256,512]{2,1,0:T(8,128)(2,1)S(1)} %collective-permute-done.2), channel_id=1, source_target_pairs={{0,1},{1,2},{2,3},{3,4},{4,5},{5,6},{6,7},{7,0},{8,9},{9,10},{10,1... | collective-permute-start | bytes 786440 | tf_op jit(solution)/shard_map/ppermute | solution.py:16
  57.6 18.6 %copy-start.6 = (bf16[1,256,512]{2,1,0:T(8,128)(2,1)}, bf16[1,256,512]{2,1,0:T(8,128)(2,1)S(1)}, u32[]{:S(2)}) copy-start(bf16[1,256,512]{2,1,0:T(8,128)(2,1)S(1)} %collective-permute-done.3) | copy-start | bytes 786436
  57.6 9.2 %collective-permute-start.4 = (bf16[1,256,512]{2,1,0:T(8,128)(2,1)S(1)}, bf16[1,256,512]{2,1,0:T(8,128)(2,1)}, u32[]{:S(2)}, u32[]{:S(2)}) collective-permute-start(bf16[1,256,512]{2,1,0:T(8,128)(2,1)S(1)} %collective-permute-done.3), channel_id=1, source_target_pairs={{0,1},{1,2},{2,3},{3,4},{4,5},{5,6},{6,7},{7,0},{8,9},{9,10},{10,1... | collective-permute-start | bytes 786440 | tf_op jit(solution)/shard_map/ppermute | solution.py:16
  66.8 9.4 %collective-permute-start.5 = (bf16[1,256,512]{2,1,0:T(8,128)(2,1)}, bf16[1,256,512]{2,1,0:T(8,128)(2,1)}, u32[]{:S(2)}, u32[]{:S(2)}) collective-permute-start(bf16[1,256,512]{2,1,0:T(8,128)(2,1)} %collective-permute-done.4), channel_id=1, source_target_pairs={{0,1},{1,2},{2,3},{3,4},{4,5},{5,6},{6,7},{7,0},{8,9},{9,10},{10,1... | collective-permute-start | bytes 786440 | tf_op jit(solution)/shard_map/ppermute | solution.py:16
  76.2 9.4 %collective-permute-start.6 = (bf16[1,256,512]{2,1,0:T(8,128)(2,1)}, bf16[1,256,512]{2,1,0:T(8,128)(2,1)}, u32[]{:S(2)}, u32[]{:S(2)}) collective-permute-start(bf16[1,256,512]{2,1,0:T(8,128)(2,1)} %collective-permute-done.5), channel_id=1, source_target_pairs={{0,1},{1,2},{2,3},{3,4},{4,5},{5,6},{6,7},{7,0},{8,9},{9,10},{10,1... | collective-permute-start | bytes 786440 | tf_op jit(solution)/shard_map/ppermute | solution.py:16
  81.3 13.1 %copy-start.7 = (bf16[1,256,512]{2,1,0:T(8,128)(2,1)S(1)}, bf16[1,256,512]{2,1,0:T(8,128)(2,1)}, u32[]{:S(2)}) copy-start(bf16[1,256,512]{2,1,0:T(8,128)(2,1)} %copy-done.6) | copy-start | bytes 786436
  81.3 13.1 %copy-start.5 = (bf16[1,256,512]{2,1,0:T(8,128)(2,1)S(1)}, bf16[1,256,512]{2,1,0:T(8,128)(2,1)}, u32[]{:S(2)}) copy-start(bf16[1,256,512]{2,1,0:T(8,128)(2,1)} %copy-done.4) | copy-start | bytes 786436
  81.3 13.1 %copy-start.3 = (bf16[1,256,512]{2,1,0:T(8,128)(2,1)S(1)}, bf16[1,256,512]{2,1,0:T(8,128)(2,1)}, u32[]{:S(2)}) copy-start(bf16[1,256,512]{2,1,0:T(8,128)(2,1)} %copy-done.2) | copy-start | bytes 786436
  130.8 7.5 %copy-start.8 = (bf16[512,4,64]{0,2,1:T(8,128)(2,1)S(1)}, bf16[512,4,64]{0,2,1:T(8,128)(2,1)}, u32[]{:S(2)}) copy-start(bf16[512,4,64]{0,2,1:T(8,128)(2,1)} %get-tuple-element.64) | copy-start | bytes 786436
  148.9 20.8 %copy-start.9 = (f32[1024]{0:T(1024)S(1)}, f32[1024]{0:T(1024)}, u32[]{:S(2)}) copy-start(f32[1024]{0:T(1024)} %param.23) | copy-start | bytes 12292
  170.5 44.3 %reduce-scatter.2.cloned.1.call-start = ((), (), s32[]{:S(2)}) async-start(), calls=%async_computation.4 | async-start | bytes 1310720 | tf_op jit(solution)/shard_map/reduce_scatter | solution.py:158
Sparse Core Ops, SparseCore 0:
  14.5 17.0 all-gather.2
  170.6 13.7 all-gather.4
  189.8 24.8 reduce-scatter.1
